TPU v7x, 32 devices: a whole 2x2x4 slice. The times are simulated.
32 devices in a mesh: rows: 16 (over z, y, x), tok: 2 (over core).
Axes of the slice: x: 2, y: 2, z: 4, core: 2. Of those that a mesh axis runs over, the one named last changes fastest.
Arguments:
- calib: bfloat16 [128, 26752], P('tok'), may hold values from -6 to 6
- w_panels: bfloat16 [16384, 256], P(('rows', 'tok')), may hold values from -0.0390625 to 0.0390625
- w_trail: bfloat16 [16384, 26496], P(('rows', 'tok')), may hold values from -0.0390625 to 0.0390625
- keep_mask: int32 [16384, 256], P(('rows', 'tok')), may hold values from 0 to 1, as said below
- factor_block: float32 [256, 256], replicated, as said below
- factor_trail: bfloat16 [256, 26496], P(None, 'rows'), may hold values from -0.359375 to 0.359375
Outputs:
- pruned: bfloat16 [16384, 256], P(('rows', 'tok'))
- next_input: bfloat16 [128, 16384], replicated
Inputs may be any that keep to these rules, and one draw needn't show every extreme that they name: `keep_mask`: in every row, each aligned group of 4 columns holds exactly two ones. `factor_block`: upper triangular, diagonal entries between 0.6 and 1.4.
All inputs are finite; a program needn't handle non-finite values.
Results may differ from a plain program's by a relative error of at most 0.001.
Values may be sent and summed in bfloat16 or wider, within the bound.
A program may use at most 192 MiB of HBM per device.

v0:
```python
import math

import jax
import jax.numpy as jnp
from jax import lax
from jax.sharding import PartitionSpec as P


def sweep_columns(current, keep_part, factor):
    column_count = factor.shape[0]
    width = math.gcd(16, column_count)
    block_count = column_count // width
    errors = jnp.zeros(current.shape, jnp.float32)
    dropped = 1.0 - keep_part.astype(jnp.float32)
    column_ids = lax.broadcasted_iota(jnp.int32, (1, column_count), 1)

    def advance(block, state_pair):
        weights_now, errors_now = state_pair
        start = (jnp.asarray(block) * width).astype(jnp.int32)
        piece = lax.dynamic_slice_in_dim(weights_now, start, width, 1)
        drop_piece = lax.dynamic_slice_in_dim(dropped, start, width, 1)
        factor_rows = lax.dynamic_slice_in_dim(factor, start, width, 0)
        local_factor = lax.dynamic_slice_in_dim(factor_rows, start, width, 1)
        column_errors = []
        for inner in range(width):
            col_error = drop_piece[:, inner] * piece[:, inner] / local_factor[inner, inner]
            piece = piece - col_error[:, None] * local_factor[inner][None, :]
            column_errors.append(col_error)
        block_errors = jnp.stack(column_errors, axis=1)
        beyond = (column_ids >= start + width).astype(jnp.float32)
        weights_now = weights_now - jnp.dot(
            block_errors, factor_rows * beyond, precision=lax.Precision.HIGHEST
        )
        weights_now = lax.dynamic_update_slice_in_dim(weights_now, piece, start, 1)
        errors_now = lax.dynamic_update_slice_in_dim(errors_now, block_errors, start, 1)
        return (weights_now, errors_now)

    return lax.fori_loop(0, block_count, advance, (current, errors))


def per_device(calib, w_panels, w_trail, keep_mask, factor_block, factor_trail):
    span_total = factor_block.shape[0]
    half_span = span_total // 2
    contract = (((1,), (1,)), ((), ()))
    tokens_all = lax.all_gather(calib, "tok", axis=0, tiled=True)
    current = w_panels.astype(jnp.float32)
    first_part, first_errors = sweep_columns(
        current[:, :half_span], keep_mask[:, :half_span], factor_block[:half_span, :half_span]
    )
    second_start = current[:, half_span:] - jnp.dot(
        first_errors, factor_block[:half_span, half_span:], precision=lax.Precision.HIGHEST
    )
    second_part, second_errors = sweep_columns(
        second_start, keep_mask[:, half_span:], factor_block[half_span:, half_span:]
    )
    current = jnp.concatenate([first_part, second_part], axis=1)
    errors = jnp.concatenate([first_errors, second_errors], axis=1)
    final_weights = current * keep_mask.astype(jnp.float32)
    x_panel = tokens_all[:, :span_total].astype(jnp.float32)
    part_panel = lax.dot_general(x_panel, final_weights, contract, precision=lax.Precision.HIGHEST)
    factor_piece = lax.all_gather(factor_trail, "rows", axis=1, tiled=True)
    piece_width = factor_piece.shape[1]
    weight_cols = w_trail.astype(jnp.float32)
    updated = weight_cols - jnp.dot(
        errors, factor_piece.astype(jnp.float32), precision=lax.Precision.HIGHEST
    )
    input_cols = lax.dynamic_slice_in_dim(tokens_all, span_total, piece_width, 1).astype(
        jnp.float32
    )
    part_trail = lax.dot_general(input_cols, updated, contract, precision=lax.Precision.HIGHEST)
    local_out = (part_panel + part_trail).astype(jnp.bfloat16)
    next_input = lax.all_gather(local_out, ("rows", "tok"), axis=1, tiled=True)
    return (final_weights.astype(jnp.bfloat16), next_input)


def solution(mesh):
    placed = (
        P("tok", None),
        P(("rows", "tok"), None),
        P(("rows", "tok"), None),
        P(("rows", "tok"), None),
        P(),
        P(None, "rows"),
    )
    return jax.shard_map(
        per_device,
        mesh=mesh,
        in_specs=placed,
        out_specs=(P(("rows", "tok"), None), P()),
        check_vma=False,
    )
```

profile of v0, /device:TPU:0, one launch (start us, length us, event | category | flops | bytes accessed | tf_op | source)
XLA Modules:
  0.0 433.4 jit_solution(1629846742756825716)
XLA Ops:
  8.7 0.9 slice.1598
  9.6 1.0 convert_element_type.65
  10.6 1.1 fusion.95
  11.9 0.9 fusion.96
  12.9 124.5 %while.38 = (s32[]{:T(128)}, f32[512,128]{0,1:T(8,128)S(1)}, f32[512,128]{0,1:T(8,128)S(1)}, f32[512,128]{0,1:T(8,128)S(1)}, f32[128,128]{1,0:T(8,128)S(1)}, /*i...) while((s32[]{:T(128)}, f32[512,128]{0,1:T(8,128)S(1)}, ...), condition=%wide.region_1.0_spmd.clone, body=%wide.region_0.0_spmd.clone.sunk | while | flops 14895398 | bytes 3314271 | solution.py:38
  26.9 1.1 dynamic_update_slice.55
  42.1 1.5 dynamic_update_slice.55
  57.7 1.5 dynamic_update_slice.55
  73.3 1.5 dynamic_update_slice.55
  88.9 1.5 dynamic_update_slice.55
  104.5 1.5 dynamic_update_slice.55
  120.1 1.5 dynamic_update_slice.55
  135.8 1.5 dynamic_update_slice.55
  137.4 1.4 convolution_subtract_fusion.2
  139.1 125.1 %while.39 = (s32[]{:T(128)}, f32[512,128]{0,1:T(8,128)S(1)}, f32[512,128]{0,1:T(8,128)S(1)}, f32[512,128]{0,1:T(8,128)S(1)}, f32[128,128]{1,0:T(8,128)S(1)}, /*i...) while((s32[]{:T(128)}, f32[512,128]{0,1:T(8,128)S(1)}, ...), condition=%wide.region_3.0_spmd.clone, body=%wide.region_2.0_spmd.clone.sunk | while | flops 14895398 | bytes 3314271 | solution.py:38
  139.2 0.8 fusion.163
  153.2 1.1 dynamic_update_slice.57
  154.5 0.8 fusion.163
  168.5 1.5 dynamic_update_slice.57
  184.2 1.5 dynamic_update_slice.57
  199.9 1.5 dynamic_update_slice.57
  201.5 0.8 fusion.163
  215.6 1.5 dynamic_update_slice.57
  231.3 1.5 dynamic_update_slice.57
  232.9 0.8 fusion.163
  247.0 1.5 dynamic_update_slice.57
  262.7 1.5 dynamic_update_slice.57
  264.6 54.7 %fusion.84 = f32[512,26496]{1,0:T(8,128)} fusion(bf16[256,26496]{0,1:T(8,128)(2,1)} %all-gather.6.cloned.1.call-done, f32[512,128]{0,1:T(8,128)S(1)} %get-tuple-element.351, f32[512,128]{0,1:T(8,128)S(1)} %get-tuple-element.349), kind=kOutput, calls=%fused_computation.189 | convolution fusion | flops 41674735616 | bytes 68354048 | tf_op jit(solution)/shard_map/dot_general | solution.py:64
  319.3 34.4 %fusion.78 = f32[512,128]{1,0:T(8,128)S(1)} fusion(f32[512,26496]{1,0:T(8,128)} %fusion.84, bf16[512,26496]{1,0:T(8,128)(2,1)} %param.12, bf16[128,26752]{1,0:T(8,128)(2,1)} %all-gather.4.cloned.1.call-done), kind=kOutput, calls=%fused_computation.180 | convolution fusion | flops 20864434176 | bytes 88440832 | tf_op jit(solution)/shard_map/dot_general | solution.py:70
  353.7 1.9 fusion.83
  356.4 64.1 %all-gather.8.cloned.1.call-done = bf16[128,16384]{0,1:T(8,128)(2,1)} async-done(((bf16[128,512]{0,1:T(8,128)(2,1)}), bf16[128,16384]{0,1:T(8,128)(2,1)}) %all-gather.8.cloned.1.call-update) | async-done | bytes 4194320 | tf_op jit(solution)/shard_map/all_gather | solution.py:72
  420.5 6.4 %copy.55 = bf16[128,16384]{1,0:T(8,128)(2,1)} copy(bf16[128,16384]{0,1:T(8,128)(2,1)} %all-gather.8.cloned.1.call-done) | data formatting | bytes 8388608
  (673 shorter events, 221.5 us)
Async XLA Ops:
  7.2 257.4 %all-gather.6.cloned.1.call-start = ((), (), s32[]{:S(2)}) async-start(), calls=%async_computation.1 | async-start | bytes 14413824 | tf_op jit(solution)/shard_map/all_gather | solution.py:61
  7.9 311.4 %all-gather.4.cloned.1.call-start = ((), (), s32[]{:S(2)}) async-start(), calls=%async_computation | async-start | bytes 10272768 | tf_op jit(solution)/shard_map/all_gather | solution.py:45
  8.6 411.9 %all-gather.8.cloned.1.call-start = ((), (), s32[]{:S(2)}) async-start(), calls=%async_computation.2 | async-start | bytes 4325376 | tf_op jit(solution)/shard_map/all_gather | solution.py:72
  319.3 34.4 %copy-start = (s32[512,256]{1,0:T(8,128)S(1)}, s32[512,256]{1,0:T(8,128)}, u32[]{:S(2)}) copy-start(s32[512,256]{1,0:T(8,128)} %param.13) | copy-start | bytes 1572868
Sparse Core Ops, SparseCore 0:
  10.8 164.1 all-gather.5
  176.5 15.7 all-gather.3
  355.8 64.7 all-gather.7
where the time goes:
time: 436 us; the launch traced here: 433 us
  other arithmetic  191 us (44%)
  matrix products  102 us (23%)
  waiting for transfers between devices  65.6 us (15%)
  local copies, waits for them, and re-layouts  54.9 us (13%)
  between operations  13.9 us (3%)
  loops' own time  5.57 us (1%)
    div x256, other arithmetic, advance(): drop_piece[:, inner] * piece[:, inner] / local_factor[inner, inner]  165 us
    all_gather x1, waiting for transfers between devices, per_device(): next_input = lax.all_gather(local_out, ('rows', 'tok'), axis=1, tiled=True)  64.1 us
    dot_general x1, matrix products, per_device(): jnp.dot(errors, factor_piece.astype(jnp.float32), precision=lax.Precision...  54.7 us
    dot_general x1, matrix products, per_device(): lax.dot_general(input_cols, updated, contract, precision=lax.Precision.HI...  34.4 us
    sub x256, other arithmetic, advance(): piece = piece - col_error[:, None] * local_factor[inner][None, :]  24.6 us
    dynamic_update_slice x16, local copies, waits for them, and re-layouts, advance(): weights_now = lax.dynamic_update_slice_in_dim(weights_now, piece, start, 1)  22.5 us
    slice x16, local copies, waits for them, and re-layouts, advance(): local_factor[inner, inner]  12.6 us
    dot_general x16, matrix products, advance(): jnp.dot(block_errors, factor_rows * beyond, precision=lax.Precision.HIGHEST)  9.59 us
  transfers between devices with their start and end apart: 3, of which 1 were waited for; matrix products, arithmetic and copies ran while one was open for 71% of the time, Pallas kernels for 0%

commit v1 on v0

v1 whole, which is shorter than its diff:
```python
import functools

import jax
import jax.numpy as jnp
from jax import lax
from jax.experimental import pallas as pl
from jax.experimental.pallas import tpu as pltpu
from jax.sharding import PartitionSpec as P

F32, BF16 = jnp.float32, jnp.bfloat16
SUPER = 64
NT = (((1,), (1,)), ((), ()))


def split(value):
    high = value.astype(BF16)
    return high, (value - high.astype(F32)).astype(BF16)


def sweep_kernel(w_ref, keep_ref, factor_ref, pruned_ref, sides_ref, cur, scale, errs):
    span = factor_ref.shape[0]
    factor = factor_ref[...]
    on_diag = lax.broadcasted_iota(jnp.int32, factor.shape, 0) == lax.broadcasted_iota(
        jnp.int32, factor.shape, 1
    )
    diagonal = jnp.sum(jnp.where(on_diag, factor, 0.0), axis=1, keepdims=True)
    factor_t = factor.T
    high, low = split(factor_t)
    cur[...] = w_ref[...].astype(F32).T
    dropped = 1.0 - keep_ref[...].astype(F32).T
    scale[...] = dropped / diagonal
    for start in range(0, span, SUPER):
        stop = start + SUPER
        groups = [cur[start + g : start + g + 8, :] for g in range(0, SUPER, 8)]
        for group in range(SUPER // 8):
            base = start + group * 8
            rates = scale[base : base + 8, :]
            rows = []
            for inner in range(8):
                col = base + inner
                row = rates[inner : inner + 1, :] * groups[group][inner : inner + 1, :]
                rows.append(row)
                for g in range(group, SUPER // 8):
                    lead = factor_t[start + g * 8 : start + g * 8 + 8, col : col + 1]
                    groups[g] = groups[g] - lead * row
            errs[base : base + 8, :] = jnp.concatenate(rows, axis=0)
        for g in range(SUPER // 8):
            cur[start + g * 8 : start + g * 8 + 8, :] = groups[g]
        if stop < span:
            err_high, err_low = split(errs[start:stop, :])
            left_high, left_low = high[stop:, start:stop], low[stop:, start:stop]
            dot = functools.partial(jnp.dot, preferred_element_type=F32)
            cur[stop:, :] = cur[stop:, :] - (
                dot(left_high, err_high) + (dot(left_high, err_low) + dot(left_low, err_high))
            )
    final = cur[...] * (1.0 - dropped)
    pruned_ref[...] = final.T.astype(BF16)
    sides_ref[0], sides_ref[1] = split(final)
    sides_ref[2], sides_ref[3] = split(errs[...])


def sweep(w_panels, keep_mask, factor_block):
    rows, span = w_panels.shape
    return pl.pallas_call(
        sweep_kernel,
        out_shape=(
            jax.ShapeDtypeStruct((rows, span), BF16),
            jax.ShapeDtypeStruct((4, span, rows), BF16),
        ),
        scratch_shapes=[pltpu.VMEM((span, rows), F32)] * 3,
        compiler_params=pltpu.CompilerParams(vmem_limit_bytes=32 << 20),
    )(w_panels, keep_mask, factor_block)


def partial_projection(calib, factor_trail, span):
    width = factor_trail.shape[1]
    start = span + lax.axis_index("rows") * width
    own = lax.dynamic_slice_in_dim(calib, start, width, 1)
    return lax.dot_general(own, factor_trail, NT, preferred_element_type=F32)


def simple_device(calib, w_panels, w_trail, keep_mask, factor_block, factor_trail):
    span = factor_block.shape[0]
    tokens = lax.all_gather(calib, "tok", axis=0, tiled=True)
    partial = partial_projection(calib, factor_trail, span)
    projected = lax.all_gather(lax.psum(partial, "rows"), "tok", axis=0, tiled=True)
    pruned, sides = sweep(w_panels, keep_mask, factor_block)
    total = lax.dot_general(tokens[:, span:], w_trail, NT, preferred_element_type=F32)
    dot = functools.partial(jnp.dot, preferred_element_type=F32)
    x_panel = tokens[:, :span]
    high = lax.reduce_precision(projected, 8, 7)
    low = (projected - high).astype(BF16)
    high = high.astype(BF16)
    total = total + (dot(x_panel, sides[0]) + dot(x_panel, sides[1]))
    total = total - (dot(high, sides[2]) + (dot(high, sides[3]) + dot(low, sides[2])))
    local = total.astype(BF16)
    return pruned, lax.all_gather(local, ("rows", "tok"), axis=1, tiled=True)


def solution(mesh):
    placed = (
        P("tok", None),
        P(("rows", "tok"), None),
        P(("rows", "tok"), None),
        P(("rows", "tok"), None),
        P(),
        P(None, "rows"),
    )
    return jax.shard_map(
        simple_device,
        mesh=mesh,
        in_specs=placed,
        out_specs=(P(("rows", "tok"), None), P()),
        check_vma=False,
    )
```

time: 436 us -> 215 us (0.49)
  other arithmetic: 191 us -> 0 us
  waiting for transfers between devices: 65.6 us -> 165 us
  matrix products: 102 us -> 19 us
  local copies, waits for them, and re-layouts: 54.9 us -> 8.61 us
  loops' own time: 5.57 us -> 0 us
    div x256 -> x0, other arithmetic: 165 us -> none  [advance(): drop_piece[:, inner] * piece[:, inner] / local_factor[inner, inner]]
    psum x0 -> x1, waiting for transfers between devices: none -> 101 us  [simple_device(): lax.psum(partial, 'rows')]
    dot_general x20 -> x7, matrix products: 102 us -> 19 us  [the longest x1 13.9 us: simple_device(): lax.dot_general(tokens[:, span:], w_trail, NT, preferred_element_type=F32)]
    sub x258 -> x0, other arithmetic: 24.7 us -> none  [the longest x256 24.6 us: advance(): piece = piece - col_error[:, None] * local_factor[inner][None, :]]
    dynamic_update_slice x32 -> x0, local copies, waits for them, and re-layouts: 22.6 us -> none  [the longest x16 22.5 us: advance(): weights_now = lax.dynamic_update_slice_in_dim(weights_now, piece, start, 1)]
    slice x19 -> x0, local copies, waits for them, and re-layouts: 15.5 us -> none  [the longest x16 12.6 us: advance(): local_factor[inner, inner]]
    another operation x2 -> x0, loops' own time: 5.57 us -> none  [sweep_columns(): return lax.fori_loop(0, block_count, advance, (current, errors))]
    all_gather x3 -> x2, waiting for transfers between devices: 64.2 us -> 63.2 us  [the longest x1 63.2 us: simple_device(): return (pruned, lax.all_gather(local, ('rows', 'tok'), axis=1, tiled=True))]
  transfers between devices with their start and end apart: 3 -> 3, of which waited for: 1 -> 2; matrix products, arithmetic and copies ran while one was open for 71% -> 0% of each run, Pallas kernels for 0% -> 2%
where the time goes in v1:
time: 215 us; the launch traced here: 214 us
  waiting for transfers between devices  165 us (77%)
  matrix products  19 us (9%)
  between operations  15.6 us (7%)
  local copies, waits for them, and re-layouts  8.61 us (4%)
  Pallas kernels  3.78 us (2%)
    psum x1, waiting for transfers between devices, simple_device(): lax.psum(partial, 'rows')  101 us
    all_gather x1, waiting for transfers between devices, simple_device(): return (pruned, lax.all_gather(local, ('rows', 'tok'), axis=1, tiled=True))  63.2 us
    dot_general x1, matrix products, simple_device(): lax.dot_general(tokens[:, span:], w_trail, NT, preferred_element_type=F32)  13.9 us
    unnamed x9, local copies, waits for them, and re-layouts  8.61 us
  transfers between devices with their start and end apart: 3, of which 2 were waited for; matrix products, arithmetic and copies ran while one was open for 0% of the time, Pallas kernels for 2%

profile of v1, /device:TPU:0, one launch (start us, length us, event | category | flops | bytes accessed | tf_op | source)
XLA Modules:
  0.0 214.2 jit_solution(633323064773273777)
XLA Ops:
  8.0 0.0 copy-start
  8.0 0.0 all-reduce.2.cloned.1.call-start
  8.1 1.1 copy-done
  9.2 1.9 fusion.20
  11.0 0.0 all-reduce.2.cloned.1.call-update
  11.1 0.0 all-gather.3.cloned.1.call-start
  11.1 0.5 all-gather.3.cloned.1.call-update
  11.6 0.0 all-gather.5.cloned.1.call-start
  11.7 0.0 copy-start.1
  11.7 1.0 copy-done.1
  12.7 0.0 copy-start.2
  12.7 0.9 copy-done.2
  13.7 0.0 copy-start.3
  13.7 0.9 copy-done.3
  14.6 3.8 %shard_map.77 = (bf16[512,256]{1,0:T(8,128)(2,1)}, bf16[4,256,512]{2,1,0:T(8,128)(2,1)S(1)}) custom-call(bf16[512,256]{1,0:T(8,128)(2,1)S(1)} %copy-done.2, s32[512,256]{1,0:T(8,128)S(1)} %copy-done.1, f32[256,256]{1,0:T(8,128)S(1)} %copy-done.3), custom_call_target="tpu_custom_call" | custom-call | tf_op jit(solution)/shard_map/pallas_call | solution.py:64
  18.4 101.2 %all-reduce.2.cloned.1.call-done = f32[64,256]{1,0:T(8,128)} async-done(((f32[64,256]{1,0:T(8,128)}), f32[64,256]{1,0:T(8,128)}) %all-reduce.2.cloned.1.call-update) | async-done | bytes 65552 | tf_op jit(solution)/shard_map/psum | solution.py:86
  119.6 2.1 all_gather.10
  121.7 0.2 fusion.7
  121.9 0.2 fusion.10
  122.1 0.2 fusion.5
  122.3 0.0 all-gather.3.cloned.1.call-done
  122.3 1.0 fusion.13
  123.4 13.9 %fusion = f32[128,512]{1,0:T(8,128)S(1)} fusion(bf16[512,26496]{1,0:T(8,128)(2,1)} %param.8, bf16[128,26752]{1,0:T(8,128)(2,1)} %all-gather.3.cloned.1.call-done), kind=kOutput, calls=%fused_computation | convolution fusion | flops 3472883712 | bytes 34177024 | tf_op jit(solution)/shard_map/dot_general | solution.py:88
  137.2 1.7 fusion.6
  138.9 0.0 all-gather.5.cloned.1.call-update
  139.0 63.2 %all-gather.5.cloned.1.call-done = bf16[128,16384]{1,0:T(8,128)(2,1)} async-done(((bf16[128,512]{1,0:T(8,128)(2,1)}), bf16[128,16384]{1,0:T(8,128)(2,1)}) %all-gather.5.cloned.1.call-update) | async-done | bytes 4194320 | tf_op jit(solution)/shard_map/all_gather | solution.py:97
  202.2 4.6 %copy.14 = bf16[128,16384]{1,0:T(8,128)(2,1)} copy(bf16[128,16384]{1,0:T(8,128)(2,1)} %all-gather.5.cloned.1.call-done) | data formatting | bytes 8388608
Async XLA Ops:
  8.0 1.2 copy-start
  8.0 111.6 %all-reduce.2.cloned.1.call-start = ((), (), s32[]{:S(2)}) async-start(), calls=%async_computation.1 | async-start | bytes 131072 | tf_op jit(solution)/shard_map/psum | solution.py:86
  11.1 111.3 %all-gather.3.cloned.1.call-start = ((), (), s32[]{:S(2)}) async-start(), calls=%async_computation | async-start | bytes 10272768 | tf_op jit(solution)/shard_map/all_gather | solution.py:84
  11.6 190.5 %all-gather.5.cloned.1.call-start = ((), (), s32[]{:S(2)}) async-start(), calls=%async_computation.2 | async-start | bytes 4325376 | tf_op jit(solution)/shard_map/all_gather | solution.py:97
  11.7 1.0 copy-start.1
  12.7 0.9 copy-start.2
  13.7 0.9 copy-start.3
Sparse Core Ops, SparseCore 0:
  14.9 104.6 all-reduce.1
  139.1 63.0 all-gather.4
Sparse Core Ops, SparseCore 1:
  13.1 20.1 all-gather.2

commit v2 on v1

--- a/solution.py
+++ b/solution.py
@@ -97,6 +97,273 @@
     return pruned, lax.all_gather(local, ("rows", "tok"), axis=1, tiled=True)
 
 
+def remote(src, dst, send_sem, recv_sem, rows, tok):
+    return pltpu.make_async_remote_copy(
+        src_ref=src,
+        dst_ref=dst,
+        send_sem=send_sem,
+        recv_sem=recv_sem,
+        device_id=(rows, tok),
+        device_id_type=pl.DeviceIdType.MESH,
+    )
+
+
+def main_kernel(
+    n, calib, partial, sides, w, out,
+    x, wbuf, own, parts, tile, proj,
+    w_sem, x_sem, own_sem, xs, xr, s1, r1, s2, r2, zs, zr, fs, fr, ss, sr, cs, cr,
+):
+    r, t = lax.axis_index("rows"), lax.axis_index("tok")
+    other = 1 - t
+    half, span = calib.shape[0], proj.shape[1]
+    chunks, width, wide = wbuf.shape
+    my_rows = pl.ds(pl.multiple_of(t * half, half), half)
+
+    def w_copy(k):
+        cols = pl.ds(pl.multiple_of(k * wide, 128), wide)
+        return pltpu.make_async_copy(w.at[:, cols], wbuf.at[k], w_sem.at[k])
+
+    def x_cols(k):
+        return pl.ds(pl.multiple_of(span + k * wide, 128), wide)
+
+    def x_copy(k):
+        cols = x_cols(k)
+        return remote(calib.at[:, cols], x.at[my_rows, cols], xs.at[k], xr.at[k], r, other)
+
+    def panel_copy():
+        cols = pl.ds(0, span)
+        return remote(
+            calib.at[:, cols], x.at[my_rows, cols], xs.at[chunks], xr.at[chunks], r, other
+        )
+
+    def loop(low, high, body):
+        lax.fori_loop(low, high, lambda i, c: (body(i), c)[1], 0)
+
+    x_local = pltpu.make_async_copy(calib, x.at[my_rows, :], x_sem)
+    x_local.start()
+    loop(0, chunks, lambda k: w_copy(k).start())
+
+    barrier = pltpu.get_barrier_semaphore()
+
+    def greet(i):
+        peer = lax.rem(2 * r + t + i, 2 * n)
+        pl.semaphore_signal(
+            barrier,
+            inc=1,
+            device_id=(peer // 2, lax.rem(peer, 2)),
+            device_id_type=pl.DeviceIdType.MESH,
+        )
+
+    loop(1, 2 * n, greet)
+    pl.semaphore_wait(barrier, 2 * n - 1)
+
+    def tile_at(ref, g, base):
+        return ref.at[
+            pl.ds(pl.multiple_of(base + 8 * (g // 2), 8), 8),
+            pl.ds(pl.multiple_of(128 * lax.rem(g, 2), 128), 128),
+        ]
+
+    def share(d):
+        g = lax.rem(r + d, n)
+        return remote(tile_at(partial, g, 0), parts.at[d], s1.at[d], r1.at[d], g, t)
+
+    def spread(i):
+        peer = lax.rem(2 * r + t + i, 2 * n)
+        return remote(
+            tile, tile_at(proj, r, t * half), s2.at[i], r2.at[i], peer // 2, lax.rem(peer, 2)
+        )
+
+    loop(1, n, lambda d: share(d).start())
+    loop(0, chunks, lambda k: x_copy(k).start())
+    panel_copy().start()
+    x_local.wait()
+
+    def add_chunk(k, total):
+        w_copy(k).wait()
+        x_copy(k).wait_recv()
+        return total + lax.dot_general(
+            wbuf[k], x[:, x_cols(k)], NT, preferred_element_type=F32
+        )
+
+    total = jnp.zeros((width, 2 * half), F32)
+    early = chunks // 2
+    total = lax.fori_loop(0, early, add_chunk, total)
+    loop(1, n, lambda d: share(d).wait_recv())
+    mine = tile_at(partial, r, 0)[...]
+    for d in range(1, n):
+        mine = mine + parts[d]
+    tile[...] = mine
+    loop(1, 2 * n, lambda i: spread(i).start())
+    tile_at(proj, r, t * half)[...] = mine
+    total = lax.fori_loop(early, chunks, add_chunk, total)
+    panel_copy().wait_recv()
+    loop(1, 2 * n, lambda i: spread(i).wait_recv())
+    dot = functools.partial(jnp.dot, preferred_element_type=F32)
+    x_panel = x[:, :span]
+    high, low = split(proj[...])
+    result = total.T + (dot(x_panel, sides[0]) + dot(x_panel, sides[1]))
+    result = result - (dot(high, sides[2]) + (dot(high, sides[3]) + dot(low, sides[2])))
+    own[...] = result.astype(BF16)
+
+    z, y, x_at = r // 4, lax.rem(r // 2, 2), lax.rem(r, 2)
+    depth = n // 4
+    at_y, at_x = r + 2 - 4 * y, r + 1 - 2 * x_at
+    plane = 2 * y + x_at
+
+    def region(h, row):
+        cols = pl.ds(pl.multiple_of((2 * row + t) * width, 128), width)
+        return out.at[pl.ds(h * half, half), cols]
+
+    def mine_of(h):
+        return own.at[pl.ds(h * half, half), :]
+
+    def held(kind, dz):
+        return lax.rem(z + depth - dz, depth) * 4 + kind
+
+    def first(h):
+        return at_y if h == 0 else at_x
+
+    def second(h):
+        return at_x if h == 0 else at_y
+
+    def z_send(h, dz):
+        to = lax.rem(z + dz, depth) * 4 + plane
+        return remote(mine_of(h), region(h, r), zs.at[h, dz], zr.at[h, dz], to, t)
+
+    def place(h, dz, which):
+        kind = plane if which == 0 else lax.rem(first(h), 4)
+        return held(kind, dz)
+
+    def f_send(h, dz, src=None):
+        spot = region(h, place(h, dz, 0))
+        src = spot if src is None else src
+        return remote(src, spot, fs.at[h, dz], fr.at[h, dz], first(h), t)
+
+    def s_send(h, dz, which, src=None):
+        spot = region(h, place(h, dz, which))
+        src = spot if src is None else src
+        i = which * depth + dz
+        return remote(src, spot, ss.at[h, i], sr.at[h, i], second(h), t)
+
+    def c_send(h, i, row, src=None):
+        spot = region(h, row)
+        src = spot if src is None else src
+        return remote(src, spot, cs.at[h, i], cr.at[h, i], r, other)
+
+    local = pltpu.make_async_copy(
+        own, out.at[:, pl.ds(pl.multiple_of((2 * r + t) * width, 128), width)], own_sem
+    )
+    for h in (0, 1):
+        f_send(h, 0, mine_of(h)).start()
+        s_send(h, 0, 0, mine_of(h)).start()
+        loop(1, depth, lambda dz: z_send(h, dz).start())
+        c_send(h, 0, r, mine_of(h)).start()
+    local.start()
+
+    def from_z(dz):
+        for h in (0, 1):
+            z_send(h, dz).wait_recv()
+            f_send(h, dz).start()
+            s_send(h, dz, 0).start()
+            c_send(h, dz, place(h, dz, 0)).start()
+
+    loop(1, depth, from_z)
+
+    def from_first(dz):
+        for h in (0, 1):
+            f_send(h, dz).wait_recv()
+            s_send(h, dz, 1).start()
+            c_send(h, depth + dz, place(h, dz, 1)).start()
+
+    loop(0, depth, from_first)
+
+    def from_second(dz):
+        for h in (0, 1):
+            for which in (0, 1):
+                s_send(h, dz, which).wait_recv()
+                kind = lax.rem(second(h), 4) if which == 0 else 3 - plane
+                c_send(h, (2 + which) * depth + dz, held(kind, dz)).start()
+
+    loop(0, depth, from_second)
+
+    def settle_c(i):
+        for h in (0, 1):
+            c_send(h, i, r).wait()
+
+    loop(0, 4 * depth, settle_c)
+    local.wait()
+
+    def settle(dz):
+        for h in (0, 1):
+            f_send(h, dz).wait_send()
+            s_send(h, dz, 0).wait_send()
+            s_send(h, dz, 1).wait_send()
+
+    loop(0, depth, settle)
+
+    def settle_z(dz):
+        for h in (0, 1):
+            z_send(h, dz).wait_send()
+
+    loop(1, depth, settle_z)
+    loop(1, n, lambda d: share(d).wait_send())
+    loop(1, 2 * n, lambda i: spread(i).wait_send())
+    loop(0, chunks, lambda k: x_copy(k).wait_send())
+    panel_copy().wait_send()
+
+
+def main_call(n, calib, partial, sides, w):
+    half, cols = calib.shape
+    width, trail = w.shape
+    span = cols - trail
+    tiles = trail // 128
+    chunks = next(d for d in range(8, tiles + 1) if tiles % d == 0)
+    depth = n // 4
+    dma = pltpu.SemaphoreType.DMA
+    vmem, anywhere = pl.BlockSpec(memory_space=pltpu.VMEM), pl.BlockSpec(memory_space=pl.ANY)
+    return pl.pallas_call(
+        functools.partial(main_kernel, n),
+        out_shape=jax.ShapeDtypeStruct((2 * half, 2 * n * width), BF16),
+        in_specs=[anywhere, vmem, vmem, anywhere],
+        out_specs=anywhere,
+        scratch_shapes=[
+            pltpu.VMEM((2 * half, cols), BF16),
+            pltpu.VMEM((chunks, width, trail // chunks), BF16),
+            pltpu.VMEM((2 * half, width), BF16),
+            pltpu.VMEM((n, 8, 128), F32),
+            pltpu.VMEM((8, 128), F32),
+            pltpu.VMEM((2 * half, span), F32),
+            dma((chunks,)),
+            dma,
+            dma,
+            dma((chunks + 1,)),
+            dma((chunks + 1,)),
+            dma((n,)),
+            dma((n,)),
+            dma((2 * n,)),
+            dma((2 * n,)),
+            dma((2, depth)),
+            dma((2, depth)),
+            dma((2, depth)),
+            dma((2, depth)),
+            dma((2, 2 * depth)),
+            dma((2, 2 * depth)),
+            dma((2, 4 * depth)),
+            dma((2, 4 * depth)),
+        ],
+        compiler_params=pltpu.CompilerParams(
+            collective_id=0, has_side_effects=True, vmem_limit_bytes=56 << 20
+        ),
+    )(calib, partial, sides, w)
+
+
+def kernel_device(n, calib, w_panels, w_trail, keep_mask, factor_block, factor_trail):
+    span = factor_block.shape[0]
+    partial = partial_projection(calib, factor_trail, span)
+    pruned, sides = sweep(w_panels, keep_mask, factor_block)
+    return pruned, main_call(n, calib, partial, sides, w_trail)
+
+
 def solution(mesh):
     placed = (
         P("tok", None),
@@ -106,8 +373,16 @@
         P(),
         P(None, "rows"),
     )
+    n = mesh.shape["rows"]
+
+    def per_device(calib, w_panels, *rest):
+        half, span, width = calib.shape[0], w_panels.shape[1], w_panels.shape[0]
+        fits = half * span == n * 1024 and span == 256 and width % 128 == 0 and n % 4 == 0
+        run = functools.partial(kernel_device, n) if fits else simple_device
+        return run(calib, w_panels, *rest)
+
     return jax.shard_map(
-        simple_device,
+        per_device,
         mesh=mesh,
         in_specs=placed,
         out_specs=(P(("rows", "tok"), None), P()),

time: 215 us -> 64 us (0.30)
  waiting for transfers between devices: 165 us -> 0 us
  Pallas kernels: 3.78 us -> 50.9 us
  matrix products: 19 us -> 1.87 us
  between operations: 15.6 us -> 0.66 us
    psum x1 -> x0, waiting for transfers between devices: 101 us -> none  [simple_device(): lax.psum(partial, 'rows')]
    all_gather x2 -> x0, waiting for transfers between devices: 63.2 us -> none  [the longest x1 63.2 us: simple_device(): return (pruned, lax.all_gather(local, ('rows', 'tok'), axis=1, tiled=True))]
    pallas_call x0 -> x1, Pallas kernels: none -> 47.1 us  [main_call(): pl.pallas_call(functools.partial(main_kernel, n), out_shape=jax.ShapeDtyp...]
    dot_general x6 -> x0, matrix products: 17.1 us -> none  [the longest x1 13.9 us: simple_device(): lax.dot_general(tokens[:, span:], w_trail, NT, preferred_element_type=F32)]
    unnamed x9 -> x11, local copies, waits for them, and re-layouts: 8.61 us -> 9.63 us
  transfers between devices with their start and end apart: 3 -> 0, of which waited for: 2 -> 0; matrix products, arithmetic and copies ran while one was open for 0% -> 0% of each run, Pallas kernels for 2% -> 0%
where the time goes in v2:
time: 64 us; the launch traced here: 63.1 us
  Pallas kernels  50.9 us (80%)
  local copies, waits for them, and re-layouts  9.63 us (15%)
  matrix products  1.87 us (3%)
  between operations  0.66 us (1%)
    pallas_call x1, Pallas kernels, main_call(): pl.pallas_call(functools.partial(main_kernel, n), out_shape=jax.ShapeDtyp...  47.1 us
    unnamed x11, local copies, waits for them, and re-layouts  9.63 us
    pallas_call x1, Pallas kernels, sweep(): pl.pallas_call(sweep_kernel, out_shape=(jax.ShapeDtypeStruct((rows, span)...  3.79 us
    dot_general x1, matrix products, partial_projection(): return lax.dot_general(own, factor_trail, NT, preferred_element_type=F32)  1.87 us

profile of v2, /device:TPU:0, one launch (start us, length us, event | category | flops | bytes accessed | tf_op | source)
XLA Modules:
  0.0 63.1 jit_solution(14309643706297945624)
XLA Ops:
  0.6 0.0 copy-start
  0.7 1.1 %copy-done = bf16[256,1656]{0,1:T(8,128)(2,1)S(1)} copy-done((bf16[256,1656]{0,1:T(8,128)(2,1)S(1)}, bf16[256,1656]{0,1:T(8,128)(2,1)}, u32[]{:S(2)}) %copy-start) | copy-done | bytes 847896
  1.8 1.9 %fusion.partial = f32[64,256]{1,0:T(8,128)} fusion(bf16[256,1656]{0,1:T(8,128)(2,1)S(1)} %copy-done, bf16[64,26752]{1,0:T(8,128)(2,1)} %calib.1, s32[]{:T(128)S(6)} %select_n.3), kind=kOutput, calls=%fused_computation | convolution fusion | flops 54263808 | bytes 1126404 | tf_op jit(solution)/shard_map/dot_general | solution.py:79
  3.7 0.0 copy-start.2
  3.7 1.0 %copy-done.2 = s32[512,256]{1,0:T(8,128)S(1)} copy-done((s32[512,256]{1,0:T(8,128)S(1)}, s32[512,256]{1,0:T(8,128)}, u32[]{:S(2)}) %copy-start.2) | copy-done | bytes 524312
  4.7 0.0 copy-start.3
  4.7 0.9 %copy-done.3 = bf16[512,256]{1,0:T(8,128)(2,1)S(1)} copy-done((bf16[512,256]{1,0:T(8,128)(2,1)S(1)}, bf16[512,256]{1,0:T(8,128)(2,1)}, u32[]{:S(2)}) %copy-start.3) | copy-done | bytes 262168
  5.7 0.0 copy-start.4
  5.7 0.9 %copy-done.4 = f32[256,256]{1,0:T(8,128)S(1)} copy-done((f32[256,256]{1,0:T(8,128)S(1)}, f32[256,256]{1,0:T(8,128)}, u32[]{:S(2)}) %copy-start.4) | copy-done | bytes 262168
  6.6 3.8 %shard_map.77 = (bf16[512,256]{1,0:T(8,128)(2,1)}, bf16[4,256,512]{2,1,0:T(8,128)(2,1)S(1)}) custom-call(bf16[512,256]{1,0:T(8,128)(2,1)S(1)} %copy-done.3, s32[512,256]{1,0:T(8,128)S(1)} %copy-done.2, f32[256,256]{1,0:T(8,128)S(1)} %copy-done.4), custom_call_target="tpu_custom_call" | custom-call | tf_op jit(solution)/shard_map/pallas_call | solution.py:64
  10.4 0.0 copy-start.1
  10.4 1.0 %copy-done.1 = bf16[4,256,512]{2,1,0:T(8,128)(2,1)} copy-done((bf16[4,256,512]{2,1,0:T(8,128)(2,1)}, bf16[4,256,512]{2,1,0:T(8,128)(2,1)S(1)}, u32[]{:S(2)}) %copy-start.1) | copy-done | bytes 1048600
  11.4 47.1 %shard_map.78 = bf16[128,16384]{1,0:T(8,128)(2,1)} custom-call(bf16[64,26752]{1,0:T(8,128)(2,1)} %calib.1, f32[64,256]{1,0:T(8,128)} %fusion.partial, bf16[4,256,512]{2,1,0:T(8,128)(2,1)} %copy-done.1, bf16[512,26496]{1,0:T(8,128)(2,1)} %w.1), custom_call_target="tpu_custom_call" | custom-call | tf_op jit(solution)/shard_map/pallas_call | solution.py:324
  58.5 4.6 %copy.9 = bf16[128,16384]{1,0:T(8,128)(2,1)} copy(bf16[128,16384]{1,0:T(8,128)(2,1)} %shard_map.78) | data formatting | bytes 8388608
Async XLA Ops:
  0.6 1.2 %copy-start = (bf16[256,1656]{0,1:T(8,128)(2,1)S(1)}, bf16[256,1656]{0,1:T(8,128)(2,1)}, u32[]{:S(2)}) copy-start(bf16[256,1656]{0,1:T(8,128)(2,1)} %param.11) | copy-start | bytes 2543620
  3.7 1.0 %copy-start.2 = (s32[512,256]{1,0:T(8,128)S(1)}, s32[512,256]{1,0:T(8,128)}, u32[]{:S(2)}) copy-start(s32[512,256]{1,0:T(8,128)} %keep_ref.1) | copy-start | bytes 1572868
  4.7 0.9 %copy-start.3 = (bf16[512,256]{1,0:T(8,128)(2,1)S(1)}, bf16[512,256]{1,0:T(8,128)(2,1)}, u32[]{:S(2)}) copy-start(bf16[512,256]{1,0:T(8,128)(2,1)} %w_ref.1) | copy-start | bytes 786436
  5.7 0.9 %copy-start.4 = (f32[256,256]{1,0:T(8,128)S(1)}, f32[256,256]{1,0:T(8,128)}, u32[]{:S(2)}) copy-start(f32[256,256]{1,0:T(8,128)} %factor_ref.1) | copy-start | bytes 786436
  10.4 1.0 %copy-start.1 = (bf16[4,256,512]{2,1,0:T(8,128)(2,1)}, bf16[4,256,512]{2,1,0:T(8,128)(2,1)S(1)}, u32[]{:S(2)}) copy-start(bf16[4,256,512]{2,1,0:T(8,128)(2,1)S(1)} %get-tuple-element.5.sides) | copy-start | bytes 3145732

commit v3 on v2

--- a/solution.py
+++ b/solution.py
@@ -65,10 +65,10 @@
         sweep_kernel,
         out_shape=(
             jax.ShapeDtypeStruct((rows, span), BF16),
-            jax.ShapeDtypeStruct((4, span, rows), BF16),
+            pltpu.VMEM((4, span, rows), BF16),
         ),
         scratch_shapes=[pltpu.VMEM((span, rows), F32)] * 3,
-        compiler_params=pltpu.CompilerParams(vmem_limit_bytes=32 << 20),
+        compiler_params=pltpu.CompilerParams(vmem_limit_bytes=60 << 20),
     )(w_panels, keep_mask, factor_block)
 
 
@@ -116,12 +116,16 @@
     r, t = lax.axis_index("rows"), lax.axis_index("tok")
     other = 1 - t
     half, span = calib.shape[0], proj.shape[1]
-    chunks, width, wide = wbuf.shape
+    steps, part, wide = wbuf.shape
+    chunks, width = steps // 2, 2 * part
     my_rows = pl.ds(pl.multiple_of(t * half, half), half)
 
-    def w_copy(k):
+    def w_copy(q, k):
         cols = pl.ds(pl.multiple_of(k * wide, 128), wide)
-        return pltpu.make_async_copy(w.at[:, cols], wbuf.at[k], w_sem.at[k])
+        i = q * chunks + k
+        return pltpu.make_async_copy(
+            w.at[pl.ds(q * part, part), cols], wbuf.at[i], w_sem.at[i]
+        )
 
     def x_cols(k):
         return pl.ds(pl.multiple_of(span + k * wide, 128), wide)
@@ -141,7 +145,8 @@
 
     x_local = pltpu.make_async_copy(calib, x.at[my_rows, :], x_sem)
     x_local.start()
-    loop(0, chunks, lambda k: w_copy(k).start())
+    for q in (0, 1):
+        loop(0, chunks, lambda k, q=q: w_copy(q, k).start())
 
     barrier = pltpu.get_barrier_semaphore()
 
@@ -178,16 +183,117 @@
     panel_copy().start()
     x_local.wait()
 
-    def add_chunk(k, total):
-        w_copy(k).wait()
-        x_copy(k).wait_recv()
-        return total + lax.dot_general(
-            wbuf[k], x[:, x_cols(k)], NT, preferred_element_type=F32
+    def product(q, low, high, total):
+        def add_chunk(k, total):
+            w_copy(q, k).wait()
+            if q == 0:
+                x_copy(k).wait_recv()
+            return total + lax.dot_general(
+                wbuf[q * chunks + k], x[:, x_cols(k)], NT, preferred_element_type=F32
+            )
+
+        return lax.fori_loop(low, high, add_chunk, total)
+
+    def finish(q, total):
+        dot = functools.partial(jnp.dot, preferred_element_type=F32)
+        mine = pl.ds(q * part, part)
+        x_panel = x[:, :span]
+        high, low = split(proj[...])
+        result = total.T + (dot(x_panel, sides[0, :, mine]) + dot(x_panel, sides[1, :, mine]))
+        errs_high = sides[2, :, mine]
+        result = result - (
+            dot(high, errs_high) + (dot(high, sides[3, :, mine]) + dot(low, errs_high))
         )
-
-    total = jnp.zeros((width, 2 * half), F32)
+        own[:, mine] = result.astype(BF16)
+
+    z, y, x_at = r // 4, lax.rem(r // 2, 2), lax.rem(r, 2)
+    depth = n // 4
+    at_y, at_x = r + 2 - 4 * y, r + 1 - 2 * x_at
+    plane = 2 * y + x_at
+
+    def region(v, row):
+        cols = pl.ds(pl.multiple_of((2 * row + t) * width + v // 2 * part, 128), part)
+        return out.at[pl.ds(v % 2 * half, half), cols]
+
+    def mine_of(v):
+        return own.at[pl.ds(v % 2 * half, half), pl.ds(v // 2 * part, part)]
+
+    def held(kind, dz):
+        return lax.rem(z + depth - dz, depth) * 4 + kind
+
+    def first(h):
+        return at_y if h % 2 == 0 else at_x
+
+    def second(h):
+        return at_x if h % 2 == 0 else at_y
+
+    def z_send(h, dz):
+        to = lax.rem(z + dz, depth) * 4 + plane
+        return remote(mine_of(h), region(h, r), zs.at[h, dz], zr.at[h, dz], to, t)
+
+    def place(h, dz, which):
+        kind = plane if which == 0 else lax.rem(first(h), 4)
+        return held(kind, dz)
+
+    def f_send(h, dz, src=None):
+        spot = region(h, place(h, dz, 0))
+        src = spot if src is None else src
+        return remote(src, spot, fs.at[h, dz], fr.at[h, dz], first(h), t)
+
+    def s_send(h, dz, which, src=None):
+        spot = region(h, place(h, dz, which))
+        src = spot if src is None else src
+        i = which * depth + dz
+        return remote(src, spot, ss.at[h, i], sr.at[h, i], second(h), t)
+
+    def c_send(h, i, row, src=None):
+        spot = region(h, row)
+        src = spot if src is None else src
+        return remote(src, spot, cs.at[h, i], cr.at[h, i], r, other)
+
+    local = pltpu.make_async_copy(
+        own, out.at[:, pl.ds(pl.multiple_of((2 * r + t) * width, 128), width)], own_sem
+    )
+
+    def send_own(q):
+        for h in (2 * q, 2 * q + 1):
+            f_send(h, 0, mine_of(h)).start()
+            s_send(h, 0, 0, mine_of(h)).start()
+            loop(1, depth, lambda dz, h=h: z_send(h, dz).start())
+            c_send(h, 0, r, mine_of(h)).start()
+
+    def from_z(q):
+        def body(dz):
+            for h in (2 * q, 2 * q + 1):
+                z_send(h, dz).wait_recv()
+                f_send(h, dz).start()
+                s_send(h, dz, 0).start()
+                c_send(h, dz, place(h, dz, 0)).start()
+
+        loop(1, depth, body)
+
+    def from_first(q):
+        def body(dz):
+            for h in (2 * q, 2 * q + 1):
+                f_send(h, dz).wait_recv()
+                s_send(h, dz, 1).start()
+                c_send(h, depth + dz, place(h, dz, 1)).start()
+
+        loop(0, depth, body)
+
+    def from_second(q):
+        def body(dz):
+            for h in (2 * q, 2 * q + 1):
+                for which in (0, 1):
+                    s_send(h, dz, which).wait_recv()
+                    kind = lax.rem(second(h), 4) if which == 0 else 3 - plane
+                    c_send(h, (2 + which) * depth + dz, held(kind, dz)).start()
+
+        loop(0, depth, body)
+
+    zero = jnp.zeros((part, 2 * half), F32)
     early = chunks // 2
-    total = lax.fori_loop(0, early, add_chunk, total)
+    total = product(0, 0, early, zero)
     loop(1, n, lambda d: share(d).wait_recv())
     mine = tile_at(partial, r, 0)[...]
     for d in range(1, n):
@@ -195,106 +301,33 @@
     tile[...] = mine
     loop(1, 2 * n, lambda i: spread(i).start())
     tile_at(proj, r, t * half)[...] = mine
-    total = lax.fori_loop(early, chunks, add_chunk, total)
+    total = product(0, early, chunks, total)
     panel_copy().wait_recv()
     loop(1, 2 * n, lambda i: spread(i).wait_recv())
-    dot = functools.partial(jnp.dot, preferred_element_type=F32)
-    x_panel = x[:, :span]
-    high, low = split(proj[...])
-    result = total.T + (dot(x_panel, sides[0]) + dot(x_panel, sides[1]))
-    result = result - (dot(high, sides[2]) + (dot(high, sides[3]) + dot(low, sides[2])))
-    own[...] = result.astype(BF16)
-
-    z, y, x_at = r // 4, lax.rem(r // 2, 2), lax.rem(r, 2)
-    depth = n // 4
-    at_y, at_x = r + 2 - 4 * y, r + 1 - 2 * x_at
-    plane = 2 * y + x_at
-
-    def region(h, row):
-        cols = pl.ds(pl.multiple_of((2 * row + t) * width, 128), width)
-        return out.at[pl.ds(h * half, half), cols]
-
-    def mine_of(h):
-        return own.at[pl.ds(h * half, half), :]
-
-    def held(kind, dz):
-        return lax.rem(z + depth - dz, depth) * 4 + kind
-
-    def first(h):
-        return at_y if h == 0 else at_x
-
-    def second(h):
-        return at_x if h == 0 else at_y
-
-    def z_send(h, dz):
-        to = lax.rem(z + dz, depth) * 4 + plane
-        return remote(mine_of(h), region(h, r), zs.at[h, dz], zr.at[h, dz], to, t)
-
-    def place(h, dz, which):
-        kind = plane if which == 0 else lax.rem(first(h), 4)
-        return held(kind, dz)
-
-    def f_send(h, dz, src=None):
-        spot = region(h, place(h, dz, 0))
-        src = spot if src is None else src
-        return remote(src, spot, fs.at[h, dz], fr.at[h, dz], first(h), t)
-
-    def s_send(h, dz, which, src=None):
-        spot = region(h, place(h, dz, which))
-        src = spot if src is None else src
-        i = which * depth + dz
-        return remote(src, spot, ss.at[h, i], sr.at[h, i], second(h), t)
-
-    def c_send(h, i, row, src=None):
-        spot = region(h, row)
-        src = spot if src is None else src
-        return remote(src, spot, cs.at[h, i], cr.at[h, i], r, other)
-
-    local = pltpu.make_async_copy(
-        own, out.at[:, pl.ds(pl.multiple_of((2 * r + t) * width, 128), width)], own_sem
-    )
-    for h in (0, 1):
-        f_send(h, 0, mine_of(h)).start()
-        s_send(h, 0, 0, mine_of(h)).start()
-        loop(1, depth, lambda dz: z_send(h, dz).start())
-        c_send(h, 0, r, mine_of(h)).start()
+    finish(0, total)
+    send_own(0)
+    late = chunks * 2 // 3
+    total = product(1, 0, late, zero)
+    from_z(0)
+    total = product(1, late, chunks, total)
+    finish(1, total)
+    send_own(1)
     local.start()
-
-    def from_z(dz):
-        for h in (0, 1):
-            z_send(h, dz).wait_recv()
-            f_send(h, dz).start()
-            s_send(h, dz, 0).start()
-            c_send(h, dz, place(h, dz, 0)).start()
-
-    loop(1, depth, from_z)
-
-    def from_first(dz):
-        for h in (0, 1):
-            f_send(h, dz).wait_recv()
-            s_send(h, dz, 1).start()
-            c_send(h, depth + dz, place(h, dz, 1)).start()
-
-    loop(0, depth, from_first)
-
-    def from_second(dz):
-        for h in (0, 1):
-            for which in (0, 1):
-                s_send(h, dz, which).wait_recv()
-                kind = lax.rem(second(h), 4) if which == 0 else 3 - plane
-                c_send(h, (2 + which) * depth + dz, held(kind, dz)).start()
-
-    loop(0, depth, from_second)
+    from_first(0)
+    from_z(1)
+    from_first(1)
+    from_second(0)
+    from_second(1)
 
     def settle_c(i):
-        for h in (0, 1):
+        for h in range(4):
             c_send(h, i, r).wait()
 
     loop(0, 4 * depth, settle_c)
     local.wait()
 
     def settle(dz):
-        for h in (0, 1):
+        for h in range(4):
             f_send(h, dz).wait_send()
             s_send(h, dz, 0).wait_send()
             s_send(h, dz, 1).wait_send()
@@ -302,7 +335,7 @@
     loop(0, depth, settle)
 
     def settle_z(dz):
-        for h in (0, 1):
+        for h in range(4):
             z_send(h, dz).wait_send()
 
     loop(1, depth, settle_z)
@@ -323,17 +356,17 @@
     vmem, anywhere = pl.BlockSpec(memory_space=pltpu.VMEM), pl.BlockSpec(memory_space=pl.ANY)
     return pl.pallas_call(
         functools.partial(main_kernel, n),
-        out_shape=jax.ShapeDtypeStruct((2 * half, 2 * n * width), BF16),
+        out_shape=pltpu.VMEM((2 * half, 2 * n * width), BF16),
         in_specs=[anywhere, vmem, vmem, anywhere],
-        out_specs=anywhere,
+        out_specs=vmem,
         scratch_shapes=[
             pltpu.VMEM((2 * half, cols), BF16),
-            pltpu.VMEM((chunks, width, trail // chunks), BF16),
+            pltpu.VMEM((2 * chunks, width // 2, trail // chunks), BF16),
             pltpu.VMEM((2 * half, width), BF16),
             pltpu.VMEM((n, 8, 128), F32),
             pltpu.VMEM((8, 128), F32),
             pltpu.VMEM((2 * half, span), F32),
-            dma((chunks,)),
+            dma((2 * chunks,)),
             dma,
             dma,
             dma((chunks + 1,)),
@@ -342,17 +375,17 @@
             dma((n,)),
             dma((2 * n,)),
             dma((2 * n,)),
-            dma((2, depth)),
-            dma((2, depth)),
-            dma((2, depth)),
-            dma((2, depth)),
-            dma((2, 2 * depth)),
-            dma((2, 2 * depth)),
-            dma((2, 4 * depth)),
-            dma((2, 4 * depth)),
+            dma((4, depth)),
+            dma((4, depth)),
+            dma((4, depth)),
+            dma((4, depth)),
+            dma((4, 2 * depth)),
+            dma((4, 2 * depth)),
+            dma((4, 4 * depth)),
+            dma((4, 4 * depth)),
         ],
         compiler_params=pltpu.CompilerParams(
-            collective_id=0, has_side_effects=True, vmem_limit_bytes=56 << 20
+            collective_id=0, has_side_effects=True, vmem_limit_bytes=48 << 20
         ),
     )(calib, partial, sides, w)
 
@@ -377,7 +410,7 @@
 
     def per_device(calib, w_panels, *rest):
         half, span, width = calib.shape[0], w_panels.shape[1], w_panels.shape[0]
-        fits = half * span == n * 1024 and span == 256 and width % 128 == 0 and n % 4 == 0
+        fits = half * span == n * 1024 and span == 256 and width % 256 == 0 and n % 4 == 0
         run = functools.partial(kernel_device, n) if fits else simple_device
         return run(calib, w_panels, *rest)
 

time: 64 us -> 55.8 us (0.87); the launches traced: 63.1 us -> 55.6 us
  local copies, waits for them, and re-layouts: 9.63 us -> 3.16 us
    unnamed x11 -> x3, local copies, waits for them, and re-layouts: 9.63 us -> 3.16 us
    pallas_call x1, Pallas kernels: 47.1 us -> 45.6 us  [main_call(): pl.pallas_call(functools.partial(main_kernel, n), out_shape=pltpu.VMEM((2...]
    pallas_call x1, Pallas kernels: 3.79 us -> 4.98 us  [sweep(): pl.pallas_call(sweep_kernel, out_shape=(jax.ShapeDtypeStruct((rows, span)...]
where the time goes in v3:
time: 55.8 us; the launch traced here: 55.6 us
  Pallas kernels  50.5 us (91%)
  local copies, waits for them, and re-layouts  3.16 us (6%)
  matrix products  1.25 us (2%)
  between operations  0.66 us (1%)
    pallas_call x1, Pallas kernels, main_call(): pl.pallas_call(functools.partial(main_kernel, n), out_shape=pltpu.VMEM((2...  45.6 us
    pallas_call x1, Pallas kernels, sweep(): pl.pallas_call(sweep_kernel, out_shape=(jax.ShapeDtypeStruct((rows, span)...  4.98 us
    unnamed x3, local copies, waits for them, and re-layouts  3.16 us
    dot_general x1, matrix products, partial_projection(): return lax.dot_general(own, factor_trail, NT, preferred_element_type=F32)  1.25 us

profile of v3, /device:TPU:0, one launch (start us, length us, event | category | flops | bytes accessed | tf_op | source)
XLA Modules:
  0.0 55.6 jit_solution(4855184769033584112)
XLA Ops:
  0.6 0.0 copy-start
  0.7 1.1 %copy-done = bf16[256,1656]{0,1:T(8,128)(2,1)S(1)} copy-done((bf16[256,1656]{0,1:T(8,128)(2,1)S(1)}, bf16[256,1656]{0,1:T(8,128)(2,1)}, u32[]{:S(2)}) %copy-start) | copy-done | bytes 847896
  1.8 1.2 %fusion.partial = f32[64,256]{1,0:T(8,128)S(1)} fusion(bf16[256,1656]{0,1:T(8,128)(2,1)S(1)} %copy-done, bf16[64,26752]{1,0:T(8,128)(2,1)} %calib.1, s32[]{:T(128)S(6)} %select_n.3), kind=kOutput, calls=%fused_computation | convolution fusion | flops 54263808 | bytes 1126404 | tf_op jit(solution)/shard_map/dot_general | solution.py:79
  3.0 5.0 %shard_map.77 = (bf16[512,256]{1,0:T(8,128)(2,1)}, bf16[4,256,512]{2,1,0:T(8,128)(2,1)S(1)}) custom-call(bf16[512,256]{1,0:T(8,128)(2,1)} %w_ref.1, s32[512,256]{1,0:T(8,128)} %keep_ref.1, f32[256,256]{1,0:T(8,128)} %factor_ref.1), custom_call_target="tpu_custom_call" | custom-call | tf_op jit(solution)/shard_map/pallas_call | solution.py:64
  8.0 45.6 %shard_map.78 = bf16[128,16384]{1,0:T(8,128)(2,1)S(1)} custom-call(bf16[64,26752]{1,0:T(8,128)(2,1)} %calib.1, f32[64,256]{1,0:T(8,128)S(1)} %fusion.partial, bf16[4,256,512]{2,1,0:T(8,128)(2,1)S(1)} %get-tuple-element.5.sides, bf16[512,26496]{1,0:T(8,128)(2,1)} %w.1), custom_call_target="tpu_custom_call" | custom-call | tf_op jit(solution)/shard_map/pallas_call | solution.py:357
  53.6 2.0 %copy.9 = bf16[128,16384]{1,0:T(8,128)(2,1)} copy(bf16[128,16384]{1,0:T(8,128)(2,1)S(1)} %shard_map.78) | data formatting | bytes 8388608
Async XLA Ops:
  0.6 1.2 %copy-start = (bf16[256,1656]{0,1:T(8,128)(2,1)S(1)}, bf16[256,1656]{0,1:T(8,128)(2,1)}, u32[]{:S(2)}) copy-start(bf16[256,1656]{0,1:T(8,128)(2,1)} %param.11) | copy-start | bytes 2543620

commit v4 on v3

--- a/solution.py
+++ b/solution.py
@@ -109,8 +109,8 @@
 
 
 def main_kernel(
-    n, calib, partial, sides, w, out,
-    x, wbuf, own, parts, tile, proj,
+    n, calib, partial, w, w_panels, keep, factor, out, pruned,
+    sides, cur, scale, errs, x, wbuf, own, parts, tile, proj,
     w_sem, x_sem, own_sem, xs, xr, s1, r1, s2, r2, zs, zr, fs, fr, ss, sr, cs, cr,
 ):
     r, t = lax.axis_index("rows"), lax.axis_index("tok")
@@ -181,6 +181,7 @@
     loop(1, n, lambda d: share(d).start())
     loop(0, chunks, lambda k: x_copy(k).start())
     panel_copy().start()
+    sweep_kernel(w_panels, keep, factor, pruned, sides, cur, scale, errs)
     x_local.wait()
 
     def product(q, low, high, total):
@@ -345,7 +346,7 @@
     panel_copy().wait_send()
 
 
-def main_call(n, calib, partial, sides, w):
+def main_call(n, calib, partial, w, w_panels, keep, factor):
     half, cols = calib.shape
     width, trail = w.shape
     span = cols - trail
@@ -356,10 +357,15 @@
     vmem, anywhere = pl.BlockSpec(memory_space=pltpu.VMEM), pl.BlockSpec(memory_space=pl.ANY)
     return pl.pallas_call(
         functools.partial(main_kernel, n),
-        out_shape=pltpu.VMEM((2 * half, 2 * n * width), BF16),
-        in_specs=[anywhere, vmem, vmem, anywhere],
-        out_specs=vmem,
+        out_shape=(
+            pltpu.VMEM((2 * half, 2 * n * width), BF16),
+            pltpu.VMEM((width, span), BF16),
+        ),
+        in_specs=[anywhere, vmem, anywhere, vmem, vmem, vmem],
+        out_specs=(vmem, vmem),
         scratch_shapes=[
+            pltpu.VMEM((4, span, width), BF16),
+            *[pltpu.VMEM((span, width), F32)] * 3,
             pltpu.VMEM((2 * half, cols), BF16),
             pltpu.VMEM((2 * chunks, width // 2, trail // chunks), BF16),
             pltpu.VMEM((2 * half, width), BF16),
@@ -387,14 +393,16 @@
         compiler_params=pltpu.CompilerParams(
             collective_id=0, has_side_effects=True, vmem_limit_bytes=48 << 20
         ),
-    )(calib, partial, sides, w)
+    )(calib, partial, w, w_panels, keep, factor)
 
 
 def kernel_device(n, calib, w_panels, w_trail, keep_mask, factor_block, factor_trail):
     span = factor_block.shape[0]
     partial = partial_projection(calib, factor_trail, span)
-    pruned, sides = sweep(w_panels, keep_mask, factor_block)
-    return pruned, main_call(n, calib, partial, sides, w_trail)
+    gathered, pruned = main_call(
+        n, calib, partial, w_trail, w_panels, keep_mask, factor_block
+    )
+    return pruned, gathered
 
 
 def solution(mesh):

time: 55.8 us -> 56 us (level)
  local copies, waits for them, and re-layouts: 3.16 us -> 6.8 us
  Pallas kernels: 50.5 us -> 46.9 us
    unnamed x3 -> x10, local copies, waits for them, and re-layouts: 3.16 us -> 6.8 us
    pallas_call x2 -> x1, Pallas kernels: 50.5 us -> 46.9 us  [main_call(): pl.pallas_call(functools.partial(main_kernel, n), out_shape=(pltpu.VMEM((...]
where the time goes in v4:
time: 56 us; the launch traced here: 55.7 us
  Pallas kernels  46.9 us (84%)
  local copies, waits for them, and re-layouts  6.8 us (12%)
  matrix products  1.25 us (2%)
  between operations  0.67 us (1%)
    pallas_call x1, Pallas kernels, main_call(): pl.pallas_call(functools.partial(main_kernel, n), out_shape=(pltpu.VMEM((...  46.9 us
    unnamed x10, local copies, waits for them, and re-layouts  6.8 us
    dot_general x1, matrix products, partial_projection(): return lax.dot_general(own, factor_trail, NT, preferred_element_type=F32)  1.25 us

profile of v4, /device:TPU:0, one launch (start us, length us, event | category | flops | bytes accessed | tf_op | source)
XLA Modules:
  0.0 55.7 jit_solution(18188659002103689901)
XLA Ops:
  0.6 0.0 copy-start
  0.7 1.1 %copy-done = bf16[256,1656]{0,1:T(8,128)(2,1)S(1)} copy-done((bf16[256,1656]{0,1:T(8,128)(2,1)S(1)}, bf16[256,1656]{0,1:T(8,128)(2,1)}, u32[]{:S(2)}) %copy-start) | copy-done | bytes 847896
  1.8 1.2 %fusion.partial = f32[64,256]{1,0:T(8,128)S(1)} fusion(bf16[256,1656]{0,1:T(8,128)(2,1)S(1)} %copy-done, bf16[64,26752]{1,0:T(8,128)(2,1)} %calib.1, s32[]{:T(128)S(6)} %select_n.3), kind=kOutput, calls=%fused_computation | convolution fusion | flops 54263808 | bytes 1126404 | tf_op jit(solution)/shard_map/dot_general | solution.py:79
  3.0 0.0 copy-start.1
  3.1 1.0 %copy-done.1 = s32[512,256]{1,0:T(8,128)S(1)} copy-done((s32[512,256]{1,0:T(8,128)S(1)}, s32[512,256]{1,0:T(8,128)}, u32[]{:S(2)}) %copy-start.1) | copy-done | bytes 524312
  4.1 0.0 copy-start.2
  4.1 0.9 %copy-done.2 = bf16[512,256]{1,0:T(8,128)(2,1)S(1)} copy-done((bf16[512,256]{1,0:T(8,128)(2,1)S(1)}, bf16[512,256]{1,0:T(8,128)(2,1)}, u32[]{:S(2)}) %copy-start.2) | copy-done | bytes 262168
  5.0 0.0 copy-start.3
  5.0 0.9 %copy-done.3 = f32[256,256]{1,0:T(8,128)S(1)} copy-done((f32[256,256]{1,0:T(8,128)S(1)}, f32[256,256]{1,0:T(8,128)}, u32[]{:S(2)}) %copy-start.3) | copy-done | bytes 262168
  6.0 46.9 %shard_map.77 = (bf16[128,16384]{1,0:T(8,128)(2,1)S(1)}, bf16[512,256]{1,0:T(8,128)(2,1)S(1)}) custom-call(bf16[64,26752]{1,0:T(8,128)(2,1)} %calib.1, f32[64,256]{1,0:T(8,128)S(1)} %fusion.partial, bf16[512,26496]{1,0:T(8,128)(2,1)} %w.1, bf16[512,256]{1,0:T(8,128)(2,1)S(1)} %copy-done.2, s32[512,256]{1,0:T(8,128)S(1)} %copy-done.1, f32[256,256]{1,0:T(8,128)S(1)} %copy-done.3), custom_call_target="tpu_custom_call" | custom-call | tf_op jit(solution)/shard_map/pallas_call | solution.py:358
  52.9 0.7 %copy.10 = bf16[512,256]{1,0:T(8,128)(2,1)} copy(bf16[512,256]{1,0:T(8,128)(2,1)S(1)} %get-tuple-element.6) | data formatting | bytes 524288
  53.6 2.0 %copy.11 = bf16[128,16384]{1,0:T(8,128)(2,1)} copy(bf16[128,16384]{1,0:T(8,128)(2,1)S(1)} %get-tuple-element.7) | data formatting | bytes 8388608
Async XLA Ops:
  0.6 1.2 %copy-start = (bf16[256,1656]{0,1:T(8,128)(2,1)S(1)}, bf16[256,1656]{0,1:T(8,128)(2,1)}, u32[]{:S(2)}) copy-start(bf16[256,1656]{0,1:T(8,128)(2,1)} %param.11) | copy-start | bytes 2543620
  3.0 1.0 %copy-start.1 = (s32[512,256]{1,0:T(8,128)S(1)}, s32[512,256]{1,0:T(8,128)}, u32[]{:S(2)}) copy-start(s32[512,256]{1,0:T(8,128)} %keep.1) | copy-start | bytes 1572868
  4.1 0.9 %copy-start.2 = (bf16[512,256]{1,0:T(8,128)(2,1)S(1)}, bf16[512,256]{1,0:T(8,128)(2,1)}, u32[]{:S(2)}) copy-start(bf16[512,256]{1,0:T(8,128)(2,1)} %w_panels.1) | copy-start | bytes 786436
  5.0 0.9 %copy-start.3 = (f32[256,256]{1,0:T(8,128)S(1)}, f32[256,256]{1,0:T(8,128)}, u32[]{:S(2)}) copy-start(f32[256,256]{1,0:T(8,128)} %factor.1) | copy-start | bytes 786436
